TPU v7x, 32 devices: a whole 2x2x4 slice. The times are simulated.
32 devices in a mesh: ctx: 8 (over z, y), kv: 4 (over x, core).
Axes of the slice: x: 2, y: 2, z: 4, core: 2. Of those that a mesh axis runs over, the one named last changes fastest.
Arguments:
- tokens: bfloat16 [4096, 8192], P('ctx', 'kv'), may hold values from -6 to 6
- segment_ids: int32 [4096], replicated, may hold values from 0 to 15, never falling along the last dimension, each value on 1 to 1024 neighbouring positions
- query_weight: bfloat16 [8192, 4096], P('ctx', 'kv'), may hold values from -2 to 2
- key_weight: bfloat16 [8192, 512], P('ctx', 'kv'), may hold values from -2 to 2
- value_projection_matrix: bfloat16 [8192, 512], P('ctx', 'kv'), may hold values from -0.0625 to 0.0625
Outputs:
- attended: bfloat16 [4096, 4096], P('ctx', 'kv')
Inputs may be any that keep to these rules, and one draw needn't show every extreme that they name: `segment_ids`: segment ids never fall along the sequence; each document holds 1 to 1024 tokens and one holds exactly 1024.
All inputs are finite; a program needn't handle non-finite values.
Results may differ from a plain program's by a relative error of at most 0.0085.
Values may be sent and summed in bfloat16 or wider, within the bound.
A program may use at most 128 MiB of HBM per device.

v0:
```python
import jax
import jax.numpy as jnp
from jax import lax
from jax.sharding import PartitionSpec as P

HEAD_DIMENSION = 128


def shifted(shard, axis, by):
    length = lax.axis_size(axis)
    pairs = [(i, i + by) for i in range(length) if 0 <= i + by < length]
    return lax.ppermute(shard, axis, pairs)


def attend_block(query_matrix, key_matrix, value_matrix, visible):
    head_size = query_matrix.shape[-1]
    scores = jnp.einsum(
        "thgd,shd->hgts", query_matrix, key_matrix, preferred_element_type=jnp.float32
    ) * head_size ** (-0.5)
    scores = jnp.where(visible[None, None], scores, -1e30)
    largest = jnp.max(scores, axis=-1, keepdims=True)
    expon = jnp.where(visible[None, None], jnp.exp(scores - largest), 0.0)
    total = jnp.sum(expon, axis=-1, keepdims=True)
    weights = expon.astype(jnp.bfloat16)
    summed = jnp.einsum("hgts,shd->hgtd", weights, value_matrix, preferred_element_type=jnp.float32)
    result = summed / total
    rows = query_matrix.shape[0]
    return jnp.transpose(result, (2, 0, 1, 3)).reshape(rows, -1).astype(jnp.bfloat16)


def shards(tokens, segment_ids, query_weight, key_weight, value_projection_matrix):
    whole = lax.all_gather(tokens, "kv", axis=1, tiled=True)
    rows = whole.shape[0]

    def add_rows(piece):
        return jnp.dot(whole, piece, preferred_element_type=jnp.float32)

    q_sum = add_rows(lax.all_gather(query_weight, "ctx", axis=0, tiled=True))
    k_sum = add_rows(lax.all_gather(key_weight, "ctx", axis=0, tiled=True))
    v_sum = add_rows(lax.all_gather(value_projection_matrix, "ctx", axis=0, tiled=True))
    query_rows = q_sum.astype(jnp.bfloat16)
    key_rows = k_sum.astype(jnp.bfloat16)
    value_rows = v_sum.astype(jnp.bfloat16)
    prev_key, prev_value = shifted((key_rows, value_rows), "ctx", 1)
    kv_heads = key_weight.shape[1] // HEAD_DIMENSION
    query_group = query_weight.shape[1] // (HEAD_DIMENSION * kv_heads)
    query_matrix = query_rows.reshape(rows, kv_heads, query_group, HEAD_DIMENSION)
    nearby_keys = jnp.concatenate([prev_key, key_rows], axis=0).reshape(
        2 * rows, kv_heads, HEAD_DIMENSION
    )
    nearby_values = jnp.concatenate([prev_value, value_rows], axis=0).reshape(
        2 * rows, kv_heads, HEAD_DIMENSION
    )
    position = lax.axis_index("ctx")
    begin_offset = position * rows
    prev_start = jnp.maximum(begin_offset - rows, 0)
    seg_query = lax.dynamic_slice_in_dim(segment_ids, begin_offset, rows, 0)
    seg_prev = lax.dynamic_slice_in_dim(segment_ids, prev_start, rows, 0)
    seg_keys = jnp.concatenate([seg_prev, seg_query], axis=0)
    qpos = begin_offset + jnp.arange(rows, dtype=jnp.int32)
    kpos = begin_offset - rows + jnp.arange(2 * rows, dtype=jnp.int32)
    visible = (kpos[None, :] <= qpos[:, None]) & (kpos[None, :] > qpos[:, None] - rows)
    visible = visible & (kpos[None, :] >= 0) & (seg_keys[None, :] == seg_query[:, None])
    return attend_block(query_matrix, nearby_keys, nearby_values, visible)


def solution(mesh):
    placed = (P("ctx", "kv"), P(), P("ctx", "kv"), P("ctx", "kv"), P("ctx", "kv"))
    return jax.shard_map(
        shards, mesh=mesh, in_specs=placed, out_specs=P("ctx", "kv"), check_vma=False
    )
```

profile of v0, /device:TPU:0, one launch (start us, length us, event | category | flops | bytes accessed | tf_op | source)
XLA Modules:
  0.0 434.3 jit_solution(8953648349559909561)
XLA Ops:
  6.5 0.0 all-gather.11.cloned.1.call-start
  6.5 0.7 all-gather.11.cloned.1.call-update
  7.3 0.0 all-gather.5.cloned.1.call-start
  7.3 0.7 all-gather.5.cloned.1.call-update
  8.0 0.0 all-gather.7.cloned.1.call-start
  8.1 0.7 all-gather.7.cloned.1.call-update
  8.7 0.0 all-gather.9.cloned.1.call-start
  8.8 0.5 all-gather.9.cloned.1.call-update
  9.3 0.8 fusion.22
  10.2 1.0 compare_and_fusion
  11.2 50.3 %all-gather.11.cloned.1.call-done = bf16[8192,128]{1,0:T(8,128)(2,1)} async-done(((bf16[1024,128]{1,0:T(8,128)(2,1)}), bf16[8192,128]{1,0:T(8,128)(2,1)}) %all-gather.11.cloned.1.call-update) | async-done | bytes 2097168 | tf_op jit(solution)/shard_map/all_gather | solution.py:40
  61.5 58.4 %all-gather.5.cloned.1.call-done = bf16[512,8192]{1,0:T(8,128)(2,1)} async-done(((bf16[512,2048]{1,0:T(8,128)(2,1)}), bf16[512,8192]{1,0:T(8,128)(2,1)}) %all-gather.5.cloned.1.call-update) | async-done | bytes 8388624 | tf_op jit(solution)/shard_map/all_gather | solution.py:32
  119.9 6.3 %convolution_convert_fusion.1 = bf16[512,128]{1,0:T(8,128)(2,1)S(1)} fusion(bf16[512,8192]{1,0:T(8,128)(2,1)} %all-gather.5.cloned.1.call-done, bf16[8192,128]{1,0:T(8,128)(2,1)} %all-gather.11.cloned.1.call-done), kind=kOutput, calls=%fused_computation.12 | convolution fusion | flops 1073807360 | bytes 10616832 | tf_op jit(solution)/shard_map/dot_general | solution.py:36
  126.2 3.4 collective-permute-start.1
  129.6 42.6 %all-gather.7.cloned.1.call-done = bf16[8192,128]{1,0:T(8,128)(2,1)} async-done(((bf16[1024,128]{1,0:T(8,128)(2,1)}), bf16[8192,128]{1,0:T(8,128)(2,1)}) %all-gather.7.cloned.1.call-update) | async-done | bytes 2097168 | tf_op jit(solution)/shard_map/all_gather | solution.py:39
  172.2 6.3 %convolution_convert_fusion.2 = bf16[512,128]{1,0:T(8,128)(2,1)S(1)} fusion(bf16[512,8192]{1,0:T(8,128)(2,1)} %all-gather.5.cloned.1.call-done, bf16[8192,128]{1,0:T(8,128)(2,1)} %all-gather.7.cloned.1.call-done), kind=kOutput, calls=%fused_computation.13 | convolution fusion | flops 1073807360 | bytes 10616832 | tf_op jit(solution)/shard_map/dot_general | solution.py:36
  178.5 2.6 collective-permute-start
  181.1 219.3 %all-gather.9.cloned.1.call-done = bf16[8192,1024]{1,0:T(8,128)(2,1)} async-done(((bf16[1024,1024]{1,0:T(8,128)(2,1)}), bf16[8192,1024]{1,0:T(8,128)(2,1)}) %all-gather.9.cloned.1.call-update) | async-done | bytes 16777232 | tf_op jit(solution)/shard_map/all_gather | solution.py:38
  400.4 14.8 %fusion.7 = bf16[64,8,8,128]{3,2,1,0:T(8,128)(2,1)S(1)} fusion(bf16[512,8192]{1,0:T(8,128)(2,1)} %all-gather.5.cloned.1.call-done, bf16[8192,1024]{1,0:T(8,128)(2,1)} %all-gather.9.cloned.1.call-done), kind=kOutput, calls=%fused_computation.11 | convolution fusion | flops 8590458880 | bytes 26214400 | tf_op jit(solution)/shard_map/dot_general | solution.py:36
  415.1 0.0 collective-permute-done
  415.2 2.9 fusion
  418.1 4.0 fusion.1
  422.1 0.0 collective-permute-done.1
  422.1 4.3 divide_convert_fusion
  426.4 1.3 copy.9
  (3 shorter events, 0.0 us)
Async XLA Ops:
  6.5 55.0 %all-gather.11.cloned.1.call-start = ((), (), s32[]{:S(2)}) async-start(), calls=%async_computation.3 | async-start | bytes 2359296 | tf_op jit(solution)/shard_map/all_gather | solution.py:40
  7.3 112.6 %all-gather.5.cloned.1.call-start = ((), (), s32[]{:S(2)}) async-start(), calls=%async_computation | async-start | bytes 10485760 | tf_op jit(solution)/shard_map/all_gather | solution.py:32
  8.0 164.1 %all-gather.7.cloned.1.call-start = ((), (), s32[]{:S(2)}) async-start(), calls=%async_computation.1 | async-start | bytes 2359296 | tf_op jit(solution)/shard_map/all_gather | solution.py:39
  8.7 391.6 %all-gather.9.cloned.1.call-start = ((), (), s32[]{:S(2)}) async-start(), calls=%async_computation.2 | async-start | bytes 18874368 | tf_op jit(solution)/shard_map/all_gather | solution.py:38
  126.2 295.9 %collective-permute-start.1 = (bf16[512,128]{1,0:T(8,128)(2,1)S(1)}, bf16[512,128]{1,0:T(8,128)(2,1)S(1)}, u32[]{:S(2)}, u32[]{:S(2)}) collective-permute-start(bf16[512,128]{1,0:T(8,128)(2,1)S(1)} %convolution_convert_fusion.1), channel_id=1, source_target_pairs={{0,4},{4,8},{8,12},{12,16},{16,20},{20,24},{24,28},{1,5},{5,9},{9,... | collective-permute-start | bytes 393224 | tf_op jit(solution)/shard_map/ppermute | solution.py:12
  178.5 236.7 %collective-permute-start = (bf16[512,128]{1,0:T(8,128)(2,1)S(1)}, bf16[512,128]{1,0:T(8,128)(2,1)S(1)}, u32[]{:S(2)}, u32[]{:S(2)}) collective-permute-start(bf16[512,128]{1,0:T(8,128)(2,1)S(1)} %convolution_convert_fusion.2), channel_id=1, source_target_pairs={{0,4},{4,8},{8,12},{12,16},{16,20},{20,24},{24,28},{1,5},{5,9},{9,... | collective-permute-start | bytes 393224 | tf_op jit(solution)/shard_map/ppermute | solution.py:12
Sparse Core Ops, SparseCore 0:
  9.5 51.9 all-gather.10
  63.1 56.7 all-gather.4
  122.0 50.1 all-gather.6
  174.1 226.1 all-gather.8
where the time goes:
time: 435 us; the launch traced here: 434 us
  waiting for transfers between devices  373 us (86%)
  matrix products  34.6 us (8%)
  between operations  13.2 us (3%)
  starting transfers between devices  6.15 us (1%)
  other arithmetic  5.01 us (1%)
    all_gather x1, waiting for transfers between devices, shards(): q_sum = add_rows(lax.all_gather(query_weight, 'ctx', axis=0, tiled=True))  219 us
    all_gather x1, waiting for transfers between devices, shards(): whole = lax.all_gather(tokens, 'kv', axis=1, tiled=True)  58.4 us
    all_gather x1, waiting for transfers between devices, shards(): lax.all_gather(value_projection_matrix, 'ctx', axis=0, tiled=True)  50.3 us
    all_gather x1, waiting for transfers between devices, shards(): k_sum = add_rows(lax.all_gather(key_weight, 'ctx', axis=0, tiled=True))  42.6 us
    dot_general x3, matrix products, add_rows(): return jnp.dot(whole, piece, preferred_element_type=jnp.float32)  27.4 us
  transfers between devices with their start and end apart: 6, of which 4 were waited for; matrix products, arithmetic and copies ran while one was open for 8% of the time, Pallas kernels for 0%

commit v1 on v0

--- a/solution.py
+++ b/solution.py
@@ -4,6 +4,22 @@
 from jax.sharding import PartitionSpec as P
 
 HEAD_DIMENSION = 128
+
+
+def collect(x, axis, dim):
+    ways, here, step = (lax.axis_size(axis), lax.axis_index(axis), x.shape[dim])
+    dims = [n * ways if d == dim else n for d, n in enumerate(x.shape)]
+    full = lax.dynamic_update_slice_in_dim(jnp.zeros(dims, x.dtype), x, here * step, axis=dim)
+    going_up = going_down = x
+    for far in range(1, ways // 2 + 1):
+        going_up = lax.ppermute(going_up, axis, [(d, (d + 1) % ways) for d in range(ways)])
+        full = lax.dynamic_update_slice_in_dim(full, going_up, (here - far) % ways * step, axis=dim)
+        if 2 * far < ways:
+            going_down = lax.ppermute(going_down, axis, [(d, (d - 1) % ways) for d in range(ways)])
+            full = lax.dynamic_update_slice_in_dim(
+                full, going_down, (here + far) % ways * step, axis=dim
+            )
+    return full
 
 
 def shifted(shard, axis, by):
@@ -37,7 +53,7 @@
 
     q_sum = add_rows(lax.all_gather(query_weight, "ctx", axis=0, tiled=True))
     k_sum = add_rows(lax.all_gather(key_weight, "ctx", axis=0, tiled=True))
-    v_sum = add_rows(lax.all_gather(value_projection_matrix, "ctx", axis=0, tiled=True))
+    v_sum = add_rows(collect(value_projection_matrix, "ctx", 0))
     query_rows = q_sum.astype(jnp.bfloat16)
     key_rows = k_sum.astype(jnp.bfloat16)
     value_rows = v_sum.astype(jnp.bfloat16)

time: 435 us -> 407 us (0.936)
  waiting for transfers between devices: 373 us -> 326 us
  starting transfers between devices: 6.15 us -> 25.3 us
    all_gather x1 -> x0, waiting for transfers between devices: 50.3 us -> none  [shards(): lax.all_gather(value_projection_matrix, 'ctx', axis=0, tiled=True)]
    ppermute x0 -> x7, waiting for transfers between devices: none -> 41 us  [the longest x4 40.6 us: collect(): lax.ppermute(going_up, axis, [(d, (d + 1) % ways) for d in range(ways)])]
    all_gather x1, waiting for transfers between devices: 42.6 us -> 6.69 us  [shards(): k_sum = add_rows(lax.all_gather(key_weight, 'ctx', axis=0, tiled=True))]
    ppermute x0 -> x7, starting transfers between devices: none -> 18.3 us  [the longest x3 11.7 us: collect(): lax.ppermute(going_down, axis, [(d, (d - 1) % ways) for d in range(ways)])]
  transfers between devices with their start and end apart: 6 -> 12, of which waited for: 4 -> 8; matrix products, arithmetic and copies ran while one was open for 8% -> 9% of each run, Pallas kernels for 0% -> 0%
where the time goes in v1:
time: 407 us; the launch traced here: 406 us
  waiting for transfers between devices  326 us (80%)
  matrix products  32.1 us (8%)
  starting transfers between devices  25.3 us (6%)
  between operations  13.4 us (3%)
  other arithmetic  4.98 us (1%)
  local copies, waits for them, and re-layouts  4.65 us (1%)
    all_gather x1, waiting for transfers between devices, shards(): q_sum = add_rows(lax.all_gather(query_weight, 'ctx', axis=0, tiled=True))  216 us
    all_gather x1, waiting for transfers between devices, shards(): whole = lax.all_gather(tokens, 'kv', axis=1, tiled=True)  60 us
    ppermute x4, waiting for transfers between devices, collect(): lax.ppermute(going_up, axis, [(d, (d + 1) % ways) for d in range(ways)])  40.6 us
    dot_general x3, matrix products, add_rows(): return jnp.dot(whole, piece, preferred_element_type=jnp.float32)  24.2 us
    ppermute x3, starting transfers between devices, collect(): lax.ppermute(going_down, axis, [(d, (d - 1) % ways) for d in range(ways)])  11.7 us
  transfers between devices with their start and end apart: 12, of which 8 were waited for; matrix products, arithmetic and copies ran while one was open for 9% of the time, Pallas kernels for 0%

profile of v1, /device:TPU:0, one launch (start us, length us, event | category | flops | bytes accessed | tf_op | source)
XLA Modules:
  0.0 406.3 jit_solution(5667215179190038981)
XLA Ops:
  6.5 0.0 copy-start.1
  6.5 0.0 all-gather.6.cloned.1.call-start
  6.5 0.7 all-gather.6.cloned.1.call-update
  7.3 0.0 all-gather.4.cloned.1.call-start
  7.3 0.7 all-gather.4.cloned.1.call-update
  8.0 0.0 all-gather.8.cloned.1.call-start
  8.1 0.7 all-gather.8.cloned.1.call-update
  8.7 0.0 copy-done.1
  8.8 6.1 %collective-permute-start.2 = (bf16[1024,128]{1,0:T(8,128)(2,1)S(1)}, bf16[1024,128]{1,0:T(8,128)(2,1)S(1)}, u32[]{:S(2)}, u32[]{:S(2)}) collective-permute-start(bf16[1024,128]{1,0:T(8,128)(2,1)S(1)} %copy-done.1), channel_id=1, source_target_pairs={{0,28},{4,0},{8,4},{12,8},{16,12},{20,16},{24,20},{28,24},{1,29},{... | collective-permute-start | bytes 786440 | tf_op jit(solution)/shard_map/ppermute | solution.py:18
  14.8 0.0 collective-permute-start.1
  14.8 0.8 fusion.23
  15.7 11.0 %collective-permute-done.1 = bf16[1024,128]{1,0:T(8,128)(2,1)S(1)} collective-permute-done((bf16[1024,128]{1,0:T(8,128)(2,1)S(1)}, bf16[1024,128]{1,0:T(8,128)(2,1)S(1)}, u32[]{:S(2)}, u32[]{:S(2)}) %collective-permute-start.1) | collective-permute-done | bytes 262176 | tf_op jit(solution)/shard_map/ppermute | solution.py:15
  26.7 2.5 collective-permute-start.3
  29.1 0.9 compare_and_fusion
  30.1 0.0 collective-permute-done.2
  30.1 3.0 collective-permute-start.4
  33.1 0.3 broadcast_in_dim.35
  33.5 7.9 %collective-permute-done.3 = bf16[1024,128]{1,0:T(8,128)(2,1)} collective-permute-done((bf16[1024,128]{1,0:T(8,128)(2,1)S(1)}, bf16[1024,128]{1,0:T(8,128)(2,1)}, u32[]{:S(2)}, u32[]{:S(2)}) %collective-permute-start.3) | collective-permute-done | bytes 262176 | tf_op jit(solution)/shard_map/ppermute | solution.py:15
  41.5 1.7 collective-permute-start.5
  43.3 0.4 collective-permute-done.4
  43.6 2.7 collective-permute-start.6
  46.3 1.0 constant_dynamic-update-slice_fusion.4
  47.3 13.3 %collective-permute-done.5 = bf16[1024,128]{1,0:T(8,128)(2,1)S(1)} collective-permute-done((bf16[1024,128]{1,0:T(8,128)(2,1)}, bf16[1024,128]{1,0:T(8,128)(2,1)S(1)}, u32[]{:S(2)}, u32[]{:S(2)}) %collective-permute-start.5) | collective-permute-done | bytes 262176 | tf_op jit(solution)/shard_map/ppermute | solution.py:15
  60.6 2.4 collective-permute-start.7
  62.9 1.0 constant_dynamic-update-slice_fusion.3
  64.0 0.0 collective-permute-done.6
  64.0 8.5 %collective-permute-done.7 = bf16[1024,128]{1,0:T(8,128)(2,1)S(1)} collective-permute-done((bf16[1024,128]{1,0:T(8,128)(2,1)S(1)}, bf16[1024,128]{1,0:T(8,128)(2,1)S(1)}, u32[]{:S(2)}, u32[]{:S(2)}) %collective-permute-start.7) | collective-permute-done | bytes 262176 | tf_op jit(solution)/shard_map/ppermute | solution.py:15
  72.5 6.7 %all-gather.6.cloned.1.call-done = bf16[8192,128]{1,0:T(8,128)(2,1)} async-done(((bf16[1024,128]{1,0:T(8,128)(2,1)}), bf16[8192,128]{1,0:T(8,128)(2,1)}) %all-gather.6.cloned.1.call-update) | async-done | bytes 2097168 | tf_op jit(solution)/shard_map/all_gather | solution.py:55
  79.2 60.0 %all-gather.4.cloned.1.call-done = bf16[512,8192]{1,0:T(8,128)(2,1)} async-done(((bf16[512,2048]{1,0:T(8,128)(2,1)}), bf16[512,8192]{1,0:T(8,128)(2,1)}) %all-gather.4.cloned.1.call-update) | async-done | bytes 8388624 | tf_op jit(solution)/shard_map/all_gather | solution.py:48
  139.2 0.0 copy-start
  139.2 6.4 %convolution_convert_fusion.2 = bf16[512,128]{1,0:T(8,128)(2,1)S(1)} fusion(bf16[512,8192]{1,0:T(8,128)(2,1)} %all-gather.4.cloned.1.call-done, bf16[8192,128]{1,0:T(8,128)(2,1)} %all-gather.6.cloned.1.call-done), kind=kOutput, calls=%fused_computation.13 | convolution fusion | flops 1073807360 | bytes 10616832 | tf_op jit(solution)/shard_map/dot_general | solution.py:52
  145.7 3.4 collective-permute-start
  149.1 0.0 copy-done
  149.1 2.9 fusion.8
  152.0 3.6 collective-permute-start.8
  155.6 216.0 %all-gather.8.cloned.1.call-done = bf16[8192,1024]{1,0:T(8,128)(2,1)} async-done(((bf16[1024,1024]{1,0:T(8,128)(2,1)}), bf16[8192,1024]{1,0:T(8,128)(2,1)}) %all-gather.8.cloned.1.call-update) | async-done | bytes 16777232 | tf_op jit(solution)/shard_map/all_gather | solution.py:54
  371.6 14.8 %fusion.7 = bf16[64,8,8,128]{3,2,1,0:T(8,128)(2,1)S(1)} fusion(bf16[512,8192]{1,0:T(8,128)(2,1)} %all-gather.4.cloned.1.call-done, bf16[8192,1024]{1,0:T(8,128)(2,1)} %all-gather.8.cloned.1.call-done), kind=kOutput, calls=%fused_computation.11 | convolution fusion | flops 8590458880 | bytes 26214400 | tf_op jit(solution)/shard_map/dot_general | solution.py:52
  386.4 0.0 collective-permute-done
  386.4 2.9 fusion
  389.3 4.0 fusion.1
  393.4 0.0 collective-permute-done.8
  393.4 5.0 %divide_convert_fusion = bf16[8,512,128]{1,2,0:T(8,128)(2,1)S(1)} fusion(f32[8,512]{1,0:T(8,128)S(1)} %fusion.1, f32[1024,512,8]{1,0,2:T(8,128)S(1)} %get-tuple-element.8, f32[8,512]{1,0:T(8,128)S(1)} %get-tuple-element.7, pred[512,1024]{0,1:T(8,128)(4,1)S(1)} %compare_and_fusion, bf16[512,128]{0,1:T(8,128)(2,1)S(1)} %fusion.8, ...), kind=kOutput, calls=%fused_computation.8 | convolution fusion | flops 1096286208 | bytes 18644992 | tf_op jit(solution)/shard_map/hgts,shd->hgtd/dot_general | solution.py:41
  398.4 1.3 copy.8
  (9 shorter events, 0.3 us)
Async XLA Ops:
  6.5 2.2 copy-start.1
  6.5 72.7 %all-gather.6.cloned.1.call-start = ((), (), s32[]{:S(2)}) async-start(), calls=%async_computation.1 | async-start | bytes 2359296 | tf_op jit(solution)/shard_map/all_gather | solution.py:55
  7.3 131.9 %all-gather.4.cloned.1.call-start = ((), (), s32[]{:S(2)}) async-start(), calls=%async_computation | async-start | bytes 10485760 | tf_op jit(solution)/shard_map/all_gather | solution.py:48
  8.0 363.6 %all-gather.8.cloned.1.call-start = ((), (), s32[]{:S(2)}) async-start(), calls=%async_computation.2 | async-start | bytes 18874368 | tf_op jit(solution)/shard_map/all_gather | solution.py:54
  8.8 21.3 %collective-permute-start.2 = (bf16[1024,128]{1,0:T(8,128)(2,1)S(1)}, bf16[1024,128]{1,0:T(8,128)(2,1)S(1)}, u32[]{:S(2)}, u32[]{:S(2)}) collective-permute-start(bf16[1024,128]{1,0:T(8,128)(2,1)S(1)} %copy-done.1), channel_id=1, source_target_pairs={{0,28},{4,0},{8,4},{12,8},{16,12},{20,16},{24,20},{28,24},{1,29},{... | collective-permute-start | bytes 786440 | tf_op jit(solution)/shard_map/ppermute | solution.py:18
  14.8 11.9 %collective-permute-start.1 = (bf16[1024,128]{1,0:T(8,128)(2,1)S(1)}, bf16[1024,128]{1,0:T(8,128)(2,1)S(1)}, u32[]{:S(2)}, u32[]{:S(2)}) collective-permute-start(bf16[1024,128]{1,0:T(8,128)(2,1)S(1)} %copy-done.1), channel_id=1, source_target_pairs={{0,4},{4,8},{8,12},{12,16},{16,20},{20,24},{24,28},{28,0},{1,5},{5... | collective-permute-start | bytes 786440 | tf_op jit(solution)/shard_map/ppermute | solution.py:15
  26.7 14.8 %collective-permute-start.3 = (bf16[1024,128]{1,0:T(8,128)(2,1)S(1)}, bf16[1024,128]{1,0:T(8,128)(2,1)}, u32[]{:S(2)}, u32[]{:S(2)}) collective-permute-start(bf16[1024,128]{1,0:T(8,128)(2,1)S(1)} %collective-permute-done.1), channel_id=1, source_target_pairs={{0,4},{4,8},{8,12},{12,16},{16,20},{20,24},{24,28},{28,0},{1,5},{5... | collective-permute-start | bytes 786440 | tf_op jit(solution)/shard_map/ppermute | solution.py:15
  30.1 13.5 %collective-permute-start.4 = (bf16[1024,128]{1,0:T(8,128)(2,1)S(1)}, bf16[1024,128]{1,0:T(8,128)(2,1)}, u32[]{:S(2)}, u32[]{:S(2)}) collective-permute-start(bf16[1024,128]{1,0:T(8,128)(2,1)S(1)} %collective-permute-done.2), channel_id=1, source_target_pairs={{0,28},{4,0},{8,4},{12,8},{16,12},{20,16},{24,20},{28,24},{1,29},{... | collective-permute-start | bytes 786440 | tf_op jit(solution)/shard_map/ppermute | solution.py:18
  41.5 19.1 %collective-permute-start.5 = (bf16[1024,128]{1,0:T(8,128)(2,1)}, bf16[1024,128]{1,0:T(8,128)(2,1)S(1)}, u32[]{:S(2)}, u32[]{:S(2)}) collective-permute-start(bf16[1024,128]{1,0:T(8,128)(2,1)} %collective-permute-done.3), channel_id=1, source_target_pairs={{0,4},{4,8},{8,12},{12,16},{16,20},{20,24},{24,28},{28,0},{1,5},{5... | collective-permute-start | bytes 786440 | tf_op jit(solution)/shard_map/ppermute | solution.py:15
  43.6 20.4 %collective-permute-start.6 = (bf16[1024,128]{1,0:T(8,128)(2,1)}, bf16[1024,128]{1,0:T(8,128)(2,1)S(1)}, u32[]{:S(2)}, u32[]{:S(2)}) collective-permute-start(bf16[1024,128]{1,0:T(8,128)(2,1)} %collective-permute-done.4), channel_id=1, source_target_pairs={{0,28},{4,0},{8,4},{12,8},{16,12},{20,16},{24,20},{28,24},{1,29},{... | collective-permute-start | bytes 786440 | tf_op jit(solution)/shard_map/ppermute | solution.py:18
  60.6 11.9 %collective-permute-start.7 = (bf16[1024,128]{1,0:T(8,128)(2,1)S(1)}, bf16[1024,128]{1,0:T(8,128)(2,1)S(1)}, u32[]{:S(2)}, u32[]{:S(2)}) collective-permute-start(bf16[1024,128]{1,0:T(8,128)(2,1)S(1)} %collective-permute-done.5), channel_id=1, source_target_pairs={{0,4},{4,8},{8,12},{12,16},{16,20},{20,24},{24,28},{28,0},{1,5},{5... | collective-permute-start | bytes 786440 | tf_op jit(solution)/shard_map/ppermute | solution.py:15
  139.2 9.9 %copy-start = (bf16[512,8192]{1,0:T(8,128)(2,1)S(1)}, bf16[512,8192]{1,0:T(8,128)(2,1)}, u32[]{:S(2)}) copy-start(bf16[512,8192]{1,0:T(8,128)(2,1)} %all-gather.4.cloned.1.call-done) | copy-start | bytes 25165828
  145.7 240.7 %collective-permute-start = (bf16[512,128]{1,0:T(8,128)(2,1)S(1)}, bf16[512,128]{1,0:T(8,128)(2,1)S(1)}, u32[]{:S(2)}, u32[]{:S(2)}) collective-permute-start(bf16[512,128]{1,0:T(8,128)(2,1)S(1)} %convolution_convert_fusion.2), channel_id=1, source_target_pairs={{0,4},{4,8},{8,12},{12,16},{16,20},{20,24},{24,28},{1,5},{5,9},{9,... | collective-permute-start | bytes 393224 | tf_op jit(solution)/shard_map/ppermute | solution.py:28
  152.0 241.4 %collective-permute-start.8 = (bf16[512,128]{0,1:T(8,128)(2,1)S(1)}, bf16[512,128]{0,1:T(8,128)(2,1)S(1)}, u32[]{:S(2)}, u32[]{:S(2)}) collective-permute-start(bf16[512,128]{0,1:T(8,128)(2,1)S(1)} %fusion.8), channel_id=1, source_target_pairs={{0,4},{4,8},{8,12},{12,16},{16,20},{20,24},{24,28},{1,5},{5,9},{9,... | collective-permute-start | bytes 393224 | tf_op jit(solution)/shard_map/ppermute | solution.py:28
Sparse Core Ops, SparseCore 0:
  9.5 69.7 all-gather.5
  80.8 58.3 all-gather.3
  141.3 230.2 all-gather.7
